TPU v7x, 32 devices: a whole 2x2x4 slice. The times are simulated.
32 devices in a mesh: slab: 8 (over z, y), strip: 4 (over x, core).
Axes of the slice: x: 2, y: 2, z: 4, core: 2. Of those that a mesh axis runs over, the one named last changes fastest.
Arguments:
- colors: bfloat16 [8, 4, 16, 32, 128], P('slab', 'strip'), may hold values from -6 to 6
- transmit: bfloat16 [8, 4, 16, 128], P('slab', 'strip'), may hold values from 0.099609375 to 1
- pair_counts: int32 [4, 8, 8], P('strip'), may hold values from 0 to 2, as said below
- slot_block: int32 [4, 8, 16], P('strip'), may hold values from 0 to 1023, as said below
- assign: int32 [4, 1024], P('strip'), may hold values from 0 to 1023, as said below
- depth_rank: int32 [8], replicated, may hold values from 0 to 7, each once
- w_in: bfloat16 [256, 32], replicated, may hold values from -1 to 1
- trans_weight: bfloat16 [256], replicated, may hold values from -6 to 6
- w_mid: bfloat16 [2, 256, 256], replicated, may hold values from -0.375 to 0.375
- w_out: bfloat16 [4, 256], replicated, may hold values from -0.375 to 0.375
Outputs:
- display: bfloat16 [8, 4, 128, 4, 128], P('slab', None, 'strip')
Inputs may be any that keep to these rules, and one draw needn't show every extreme that they name: pair_counts[t, s, c] counts the span blocks renderer s of strip t sends to compositor c; in every strip one compositor gets 2 from every renderer. `slot_block`: the live slots of renderer s come first, grouped by compositor in increasing order, pair_counts[t, s, c] of them for compositor c, naming distinct blocks b with assign[t, b] // 128 = c; other slots are ignored. Each strip's row is a permutation: block b goes to compositor assign[t, b] // 128 at local position assign[t, b] % 128. `depth_rank`: a permutation.
All inputs are finite; a program needn't handle non-finite values.
Results may differ from a plain program's by a relative error of at most 0.0068.
Values may be sent and summed in bfloat16 or wider, within the bound.
No kernel may reach another device: no remote copies, remote signals or barrier semaphores. Data moves between devices by JAX's collectives and lax.ppermute only.
A program may use at most 128 MiB of HBM per device.

v0:
```python
import functools

import jax
import jax.numpy as jnp
from jax import lax
from jax.experimental import pallas as pl
from jax.experimental.pallas import tpu as pltpu
from jax.sharding import PartitionSpec as P

MOST = 2
LB = 128


EXACT_PRECISION = lax.Precision.HIGHEST


def shade_blocks(blend_color, trans_field, w_in, trans_weight, w_mid, w_out):
    summed = jnp.einsum("hf,lfp->lhp", w_in, blend_color, preferred_element_type=jnp.float32)
    summed = summed + trans_weight.astype(jnp.float32)[None, :, None] * trans_field[:, None, :]
    hidden = jax.nn.silu(summed).astype(jnp.bfloat16)
    for layer_index in range(w_mid.shape[0]):
        hidden = jax.nn.silu(
            jnp.einsum(
                "hg,lgp->lhp", w_mid[layer_index], hidden, preferred_element_type=jnp.float32
            )
        ).astype(jnp.bfloat16)
    return jnp.einsum("oh,lhp->lop", w_out, hidden, preferred_element_type=jnp.float32).astype(
        jnp.bfloat16
    )


def dense_device(
    colors, transmit, pair_counts, slot_block, assign, depth_rank, w_in, trans_weight, w_mid, w_out
):
    myself = lax.axis_index("slab")
    counts = pair_counts[0]
    blocks_all = slot_block[0]
    assign_row = assign[0]
    offsets = jnp.cumsum(counts, axis=1) - counts
    slot_rank = jnp.arange(MOST, dtype=jnp.int32)
    my_counts = lax.dynamic_index_in_dim(counts, myself, 0, keepdims=False)
    my_offsets = lax.dynamic_index_in_dim(offsets, myself, 0, keepdims=False)
    send_slots = jnp.where(
        slot_rank[None, :] < my_counts[:, None], my_offsets[:, None] + slot_rank[None, :], 0
    )
    send_color = colors[0, 0][send_slots]
    send_trans = transmit[0, 0][send_slots][:, :, None, :]
    incoming = lax.dynamic_index_in_dim(counts, myself, 1, keepdims=False)
    in_offsets = lax.dynamic_index_in_dim(offsets, myself, 1, keepdims=False)
    live_slot = slot_rank[None, :] < incoming[:, None]
    recv_slots = jnp.where(live_slot, in_offsets[:, None] + slot_rank[None, :], 0)
    recv_blocks = jnp.take_along_axis(blocks_all, recv_slots, axis=1)
    local_pos = assign_row[recv_blocks] - myself * LB
    live_flat = live_slot.reshape(-1)
    local_flat = jnp.where(live_flat, local_pos.reshape(-1), -1)
    depth_flat = jnp.repeat(depth_rank, MOST)
    ahead_table = (
        (local_flat[:, None] == local_flat[None, :])
        & (depth_flat[None, :] < depth_flat[:, None])
        & live_flat[None, :]
    )
    ahead_table = ahead_table.astype(jnp.float32)
    owner_table = (jnp.arange(LB, dtype=jnp.int32)[:, None] == local_flat[None, :]).astype(
        jnp.float32
    )
    got_color = lax.all_to_all(send_color, "slab", split_axis=0, concat_axis=0, tiled=True)
    got_trans = lax.all_to_all(send_trans, "slab", split_axis=0, concat_axis=0, tiled=True)
    pixel_count = got_color.shape[3]
    item_count = got_color.shape[0] * got_color.shape[1]
    log_trans = jnp.log(got_trans.reshape(item_count, pixel_count).astype(jnp.float32))
    log_trans = jnp.where(live_flat[:, None], log_trans, 0.0)
    front_log = jnp.dot(ahead_table, log_trans, precision=EXACT_PRECISION)
    front_share = jnp.where(live_flat[:, None], jnp.exp(front_log), 0.0)
    weighted = front_share[:, None, :] * got_color.reshape(item_count, -1, pixel_count).astype(
        jnp.float32
    )
    blend_sum = jnp.dot(owner_table, weighted.reshape(item_count, -1), precision=EXACT_PRECISION)
    blend_color = blend_sum.reshape(LB, -1, pixel_count).astype(jnp.bfloat16)
    trans_field = jnp.exp(jnp.dot(owner_table, log_trans, precision=EXACT_PRECISION))
    shaded = shade_blocks(blend_color, trans_field, w_in, trans_weight, w_mid, w_out)
    display_tiles = lax.all_to_all(shaded[None], "strip", split_axis=1, concat_axis=0, tiled=True)
    return display_tiles[None]


SMEM = pltpu.SMEM
VMEM = pltpu.VMEM
ROWS = 8
GROUP = 4


def pack_kernel(far_counts, far_colors, far_transmit, sends, counts, colors, transmit, sems):
    n_slab = sends.shape[0]
    slots, feats, span = colors.shape[2:]
    me = lax.axis_index("slab")
    copies = [
        pltpu.make_async_copy(far, near, sems.at[i])
        for i, (far, near) in enumerate(
            ((far_counts, counts), (far_transmit, transmit), (far_colors, colors))
        )
    ]
    for copy in copies:
        copy.start()
    copies[0].wait()
    mine = counts[0, pl.ds(me, 1), :].astype(jnp.float32)
    before = lax.broadcasted_iota(jnp.int32, mine.shape, 1)
    row = lax.broadcasted_iota(jnp.int32, (ROWS, slots), 0).astype(jnp.float32)
    lane = lax.broadcasted_iota(jnp.int32, (ROWS, slots), 1).astype(jnp.float32)
    offs, picks = [], []
    for c in range(n_slab):
        off = jnp.sum(jnp.where(before < c, mine, 0.0), axis=1, keepdims=True)
        offs.append(off)
        hit = (row < MOST) & (lane - row == off)
        picks.append(jnp.where(hit, 1.0, 0.0))
    pick = jnp.concatenate(picks).astype(jnp.bfloat16)
    copies[1].wait()
    tails = jnp.dot(pick, transmit[0, 0], preferred_element_type=jnp.float32)
    for c in range(n_slab):
        tail = tails[c * ROWS : (c + 1) * ROWS]
        sends[c, pl.ds(MOST * feats, ROWS), :] = tail.astype(jnp.bfloat16)
    copies[2].wait()
    for c in range(n_slab):
        off = jnp.broadcast_to(offs[c], (feats, span)).astype(jnp.bfloat16)
        for r in range(MOST):
            last = min(MOST * c + r, slots - 1)
            block = colors[0, 0, last]
            for slot in range(r, last):
                block = jnp.where(off == slot - r, colors[0, 0, slot], block)
            sends[c, pl.ds(r * feats, feats), :] = block


def plan_kernel(n_slab, slots, *refs):
    (counts, blocks, assign, depth), (rows, codes) = refs[:4], refs[4:]
    items = n_slab * MOST
    outs = codes.shape[1] // (2 * items)
    me = lax.axis_index("slab")
    row = lax.broadcasted_iota(jnp.int32, rows.shape[1:], 0)
    item_lane = lax.broadcasted_iota(jnp.int32, codes.shape, 1) // outs
    posv = jnp.zeros(rows.shape[1:], jnp.int32)
    depthv = jnp.zeros(rows.shape[1:], jnp.int32)
    firstv = jnp.zeros(rows.shape[1:], jnp.int32)
    codev = jnp.full(codes.shape, -1, jnp.int32)
    pos = []
    for s in range(n_slab):
        off = jnp.int32(0)
        for c in range(n_slab):
            off = off + jnp.where(c < me, counts[0, s, c], 0)
        count = counts[0, s, me]
        for r in range(MOST):
            i = s * MOST + r
            slot = jnp.minimum(off + r, slots - 1)
            here = assign[0, blocks[0, s, slot]] - me * LB
            here = jnp.where(r < count, here, -1)
            first = jnp.int32(i)
            for j in reversed(range(i)):
                first = jnp.where(pos[j] == here, j, first)
            pos.append(here)
            firstv = jnp.where(row == i, first, firstv)
            posv = jnp.where(row == i, here, posv)
            depthv = jnp.where(row == i, depth[s], depthv)
            codev = jnp.where(item_lane == i, jnp.where(first == i, here, -1), codev)
    rows[0] = posv
    rows[1] = depthv
    rows[2] = firstv
    codes[...] = codev.astype(jnp.float32).astype(jnp.bfloat16)


def place_kernel(w_in, trans_weight, far_out, w_first, w_out):
    feats, hidden = w_in.shape
    half_in = (w_in[...].astype(jnp.float32) * 0.5).astype(jnp.bfloat16)
    half_trans = trans_weight[...].astype(jnp.float32) * 0.5
    sub = lax.broadcasted_iota(jnp.int32, (16, hidden), 0)
    w_first[...] = jnp.zeros_like(w_first)
    for a in range(GROUP):
        w_first[a, pl.ds(a * feats, feats), :] = half_in
        tail = jnp.where(sub // 2 == a, half_trans, 0.0)
        w_first[a, pl.ds(GROUP * feats, 16), :] = tail.astype(jnp.bfloat16)
    w_out[...] = far_out[...]


def silu_half(u):
    return (u + u * jnp.tanh(u)).astype(jnp.bfloat16)


def later_layers(h, w_mid, w_out):
    for m in range(w_mid.shape[0]):
        h = silu_half(jnp.dot(h, w_mid[m], preferred_element_type=jnp.float32))
    y = lax.dot_general(
        w_out[...], h, (((1,), (1,)), ((), ())), preferred_element_type=jnp.float32
    )
    return y.astype(jnp.bfloat16).astype(jnp.float32)


def empty_kernel(trans_weight, w_mid, w_out, out):
    u = trans_weight[...].astype(jnp.float32) * 0.5
    h = silu_half(jnp.broadcast_to(u, (out.shape[1], u.shape[1])))
    y = later_layers(h, w_mid, w_out)
    outs = w_out.shape[0]
    for at in range(0, out.shape[0], outs):
        out[pl.ds(at, outs), :] = y


def shade_kernel(rows, codes, got, w_first, w_mid, w_out, out, acc, xt, ys):
    items, feats, span = acc.shape
    outs = w_out.shape[0]

    posv, depthv = rows[0], rows[1]
    front = jnp.ones((items, span), jnp.float32)
    total = jnp.ones((items, span), jnp.float32)
    for k in range(items // MOST):
        tail = got[k, pl.ds(MOST * feats, ROWS), :].astype(jnp.float32)
        for r in range(MOST):
            j = k * MOST + r
            trans_j = tail[r : r + 1, :]
            same = posv == posv[j : j + 1, :]
            total = jnp.where(same, total * trans_j, total)
            front = jnp.where(same & (depthv > depthv[j : j + 1, :]), front * trans_j, front)
    acc[...] = jnp.zeros_like(acc)
    for j in range(items):
        k, r = divmod(j, MOST)
        color = got[k, pl.ds(r * feats, feats), :].astype(jnp.float32)
        at = rows[2, j, 0]
        acc[at] = acc[at] + front[j : j + 1, :] * color
    total_hi = total.astype(jnp.bfloat16).astype(jnp.float32)
    total_lo = total - total_hi
    groups = items // GROUP
    sub = lax.broadcasted_iota(jnp.int32, (16, span), 0)
    xt[...] = jnp.zeros_like(xt)
    for q in range(groups):
        block = acc[pl.ds(q * GROUP, GROUP)].reshape(GROUP * feats, span)
        tail = jnp.zeros((16, span), jnp.float32)
        for a in range(GROUP):
            i = q * GROUP + a
            tail = jnp.where(sub == 2 * a, total_hi[i : i + 1, :], tail)
            tail = jnp.where(sub == 2 * a + 1, total_lo[i : i + 1, :], tail)
        lines = pl.ds(q * span, span)
        xt[lines, pl.ds(0, GROUP * feats)] = block.T.astype(jnp.bfloat16)
        xt[lines, pl.ds(GROUP * feats, 16)] = tail.T.astype(jnp.bfloat16)

    x = xt[...]
    stride = GROUP
    for start in range(0, GROUP, stride):
        h = jnp.concatenate(
            [
                silu_half(jnp.dot(x, w_first[a], preferred_element_type=jnp.float32))
                for a in range(start, start + stride)
            ]
        )
        y = later_layers(h, w_mid, w_out)
        for a in range(start, start + stride):
            for q in range(groups):
                at = ((a - start) * groups + q) * span
                ys[pl.ds((q * GROUP + a) * outs, outs), :] = y[:, at : at + span]
    out[pl.ds(0, items * outs), :] = ys[...].astype(jnp.bfloat16)
    out[pl.ds(items * outs, ROWS), :] = codes[...]


def join_kernel(*refs):
    *got, empty, out = refs
    _, n_strip, tile, outs, span = out.shape
    lines = tile * outs
    count = got[0].shape[0] - ROWS
    me = lax.axis_index("strip")
    want = lax.broadcasted_iota(jnp.int32, (lines, count), 0) + me * lines
    chan = lax.broadcasted_iota(jnp.int32, (lines, count), 1) % outs
    filler = jnp.concatenate([empty[...]] * (lines // ROWS))
    ones = jnp.ones((count, span), jnp.bfloat16)
    for k in range(n_strip):
        pos = got[k][pl.ds(count, ROWS), :].astype(jnp.float32)[:1, :count].astype(jnp.int32)
        hit = pos * outs + chan == want
        pick = jnp.where(hit, 1.0, 0.0).astype(jnp.bfloat16)
        blocks = got[k][pl.ds(0, count), :]
        placed = jnp.dot(pick, blocks, preferred_element_type=jnp.float32)
        filled = jnp.dot(pick, ones, preferred_element_type=jnp.float32)
        value = jnp.where(filled > 0.5, placed, filler)
        out[0, me ^ ((k + 1) % n_strip)] = value.reshape(tile, outs, span).astype(jnp.bfloat16)


def compact_device(
    n_slab,
    n_strip,
    colors,
    transmit,
    pair_counts,
    slot_block,
    assign,
    depth_rank,
    w_in,
    trans_weight,
    w_mid,
    w_out,
):
    slots, feats, span = colors.shape[2:]
    items = n_slab * MOST
    outs = w_out.shape[0]
    smem = pl.BlockSpec(memory_space=SMEM)
    vmem = pl.BlockSpec(memory_space=VMEM)
    hbm = pl.BlockSpec(memory_space=pltpu.HBM)
    small = pltpu.CompilerParams(vmem_limit_bytes=4 * 1024 * 1024)
    message = MOST * feats + ROWS
    sends = pl.pallas_call(
        pack_kernel,
        out_shape=jax.ShapeDtypeStruct((n_slab, message, span), jnp.bfloat16),
        in_specs=[hbm] * 3,
        out_specs=vmem,
        scratch_shapes=[
            pltpu.VMEM(pair_counts.shape, jnp.int32),
            pltpu.VMEM(colors.shape, colors.dtype),
            pltpu.VMEM(transmit.shape, transmit.dtype),
            pltpu.SemaphoreType.DMA((3,)),
        ],
        compiler_params=small,
        name="pack",
    )(*[pltpu.with_memory_space_constraint(a, pltpu.HBM) for a in (pair_counts, colors, transmit)])
    got = lax.all_to_all(sends, "slab", split_axis=0, concat_axis=0, tiled=True)
    hidden = w_in.shape[0]
    rough = pl.CostEstimate(flops=10**5, bytes_accessed=10**6, transcendentals=0)
    roomy = pltpu.CompilerParams(vmem_limit_bytes=16 * 1024 * 1024)
    trans_row = trans_weight[None]
    rows, codes = pl.pallas_call(
        functools.partial(plan_kernel, n_slab, slots),
        out_shape=[
            jax.ShapeDtypeStruct((3, items, span), jnp.int32),
            jax.ShapeDtypeStruct((ROWS, span), jnp.bfloat16),
        ],
        in_specs=[smem] * 4,
        out_specs=[vmem] * 2,
        compiler_params=small,
        cost_estimate=rough,
        name="plan",
    )(pair_counts, slot_block, assign, depth_rank)
    w_first, w_last = pl.pallas_call(
        place_kernel,
        out_shape=[
            jax.ShapeDtypeStruct((GROUP, 2 * GROUP * feats, hidden), jnp.bfloat16),
            jax.ShapeDtypeStruct(w_out.shape, jnp.bfloat16),
        ],
        in_specs=[vmem] * 3,
        out_specs=[vmem] * 2,
        compiler_params=small,
        cost_estimate=rough,
        name="place",
    )(w_in.T, trans_row, w_out)
    w_later = jnp.swapaxes(w_mid, 1, 2) * jnp.bfloat16(0.5)
    empty = pl.pallas_call(
        empty_kernel,
        out_shape=jax.ShapeDtypeStruct((ROWS, span), jnp.float32),
        in_specs=[vmem] * 3,
        out_specs=vmem,
        compiler_params=roomy,
        cost_estimate=rough,
        name="empty",
    )(trans_row, w_later, w_last)
    shaded = pl.pallas_call(
        shade_kernel,
        out_shape=jax.ShapeDtypeStruct((items * outs + ROWS, span), jnp.bfloat16),
        in_specs=[vmem] * 6,
        out_specs=vmem,
        scratch_shapes=[
            pltpu.VMEM((items, feats, span), jnp.float32),
            pltpu.VMEM((items // GROUP * span, 2 * GROUP * feats), jnp.bfloat16),
            pltpu.VMEM((items * outs, span), jnp.float32),
        ],
        compiler_params=roomy,
        name="shade",
    )(rows, codes, got, w_first, w_later, w_last)
    tiles = [
        lax.ppermute(shaded, "strip", [(s, s ^ k) for s in range(n_strip)])
        for k in range(1, n_strip)
    ] + [shaded]
    return pl.pallas_call(
        join_kernel,
        out_shape=jax.ShapeDtypeStruct((1, n_strip, LB // n_strip, outs, span), jnp.bfloat16),
        in_specs=[vmem] * (n_strip + 1),
        out_specs=pl.BlockSpec(),
        compiler_params=small,
        name="join",
    )(*tiles, empty)


def solution(mesh):
    n_slab, n_strip = mesh.shape["slab"], mesh.shape["strip"]
    placed = (
        P("slab", "strip", None, None, None),
        P("slab", "strip", None, None),
        P("strip", None, None),
        P("strip", None, None),
        P("strip", None),
        P(),
        P(),
        P(),
        P(),
        P(),
    )
    compact = n_strip & (n_strip - 1) == 0 and 4 * MOST * n_slab <= LB
    return jax.shard_map(
        functools.partial(compact_device, n_slab, n_strip) if compact else dense_device,
        mesh=mesh,
        in_specs=placed,
        out_specs=P("slab", None, "strip", None, None),
        check_vma=False,
    )
```

profile of v0, /device:TPU:0, one launch (start us, length us, event | category | flops | bytes accessed | tf_op | source)
XLA Modules:
  0.0 23.0 jit_solution(6988946348965380198)
XLA Ops:
  0.0 0.0 copy-start.6
  0.0 1.7 %pack.1 = bf16[8,72,128]{2,1,0:T(8,128)(2,1)} custom-call(s32[1,8,8]{2,1,0:T(8,128)} %far_counts.1, bf16[1,1,16,32,128]{4,3,2,1,0:T(8,128)(2,1)} %far_colors.1, bf16[1,1,16,128]{3,2,1,0:T(8,128)(2,1)} %far_transmit.1), custom_call_target="tpu_custom_call" | custom-call | tf_op jit(solution)/shard_map/pack/pallas_call | solution.py:300
  1.8 0.0 copy-start
  1.8 0.0 copy-start.2
  1.8 0.0 copy-start.3
  1.8 0.0 copy-start.5
  1.8 0.0 copy-start.7
  1.8 0.0 copy-start.4
  1.8 7.4 %all-to-all-start = ((bf16[8,72,128]{2,1,0:T(8,128)(2,1)}), bf16[8,72,128]{2,1,0:T(8,128)(2,1)S(1)}, u32[]{:S(2)}, u32[]{:S(2)}) async-start(bf16[8,72,128]{2,1,0:T(8,128)(2,1)} %pack.1), calls=%async_computation | async-start | bytes 294912 | tf_op jit(solution)/shard_map/all_to_all | solution.py:314
  9.2 0.0 copy-done
  9.3 0.0 copy-done.2
  9.3 0.0 copy-done.3
  9.3 0.0 copy-done.5
  9.3 0.0 copy-start.1
  9.3 0.9 %plan.1 = (s32[3,16,128]{2,1,0:T(8,128)S(1)}, bf16[8,128]{1,0:T(8,128)(2,1)S(1)}) custom-call(s32[1,8,8]{2,1,0:T(8,128)S(1)} %copy-done, s32[1,8,16]{2,1,0:T(8,128)S(1)} %copy-done.2, s32[1,1024]{1,0:T(1,128)S(1)} %copy-done.3, s32[8]{0:T(128)S(1)} %copy-done.5), custom_call_target="tpu_custom_call" | custom-call | flops 100000 | bytes 1000000 | tf_op jit(solution)/shard_map/plan/pallas_call | solution.py:319
  10.2 0.0 copy-done.7
  10.3 0.0 copy-done.4
  10.3 0.0 copy-done.1
  10.3 0.0 copy-done.6
  10.3 0.1 copy.11
  10.5 6.2 %all-to-all-done.got = bf16[8,72,128]{2,1,0:T(8,128)(2,1)S(1)} async-done(((bf16[8,72,128]{2,1,0:T(8,128)(2,1)}), bf16[8,72,128]{2,1,0:T(8,128)(2,1)S(1)}, u32[]{:S(2)}, u32[]{:S(2)}) %all-to-all-start) | async-done | bytes 147488 | tf_op jit(solution)/shard_map/all_to_all | solution.py:314
  16.7 1.6 %shade.1.refs_3_ = bf16[72,128]{1,0:T(8,128)(2,1)S(1)} custom-call(s32[3,16,128]{2,1,0:T(8,128)S(1)} %get-tuple-element.9.rows, bf16[8,128]{1,0:T(8,128)(2,1)S(1)} %get-tuple-element.10.codes, bf16[8,72,128]{2,1,0:T(8,128)(2,1)S(1)} %all-to-all-done.got, bf16[4,256,256]{2,1,0:T(8,128)(2,1)S(1)} %get-tuple-element.11.w_first, ...), custom_call_target="tpu_custom_call" | custom-call | tf_op jit(solution)/shard_map/shade/pallas_call | solution.py:353
  18.3 0.0 collective-permute-start.2
  18.3 1.6 %collective-permute-start.1 = (bf16[72,128]{1,0:T(8,128)(2,1)S(1)}, bf16[72,128]{1,0:T(8,128)(2,1)S(1)}, u32[]{:S(2)}, u32[]{:S(2)}) collective-permute-start(bf16[72,128]{1,0:T(8,128)(2,1)S(1)} %shade.1.refs_3_), channel_id=1, source_target_pairs={{0,2},{1,3},{2,0},{3,1},{4,6},{5,7},{6,4},{7,5},{8,10},{9,11},{10,... | collective-permute-start | bytes 55304 | tf_op jit(solution)/shard_map/ppermute | solution.py:367
  19.8 0.3 %collective-permute-start = (bf16[72,128]{1,0:T(8,128)(2,1)S(1)}, bf16[72,128]{1,0:T(8,128)(2,1)S(1)}, u32[]{:S(2)}, u32[]{:S(2)}) collective-permute-start(bf16[72,128]{1,0:T(8,128)(2,1)S(1)} %shade.1.refs_3_), channel_id=1, source_target_pairs={{0,1},{1,0},{2,3},{3,2},{4,5},{5,4},{6,7},{7,6},{8,9},{9,8},{10,11... | collective-permute-start | bytes 55304 | tf_op jit(solution)/shard_map/ppermute | solution.py:367
  20.1 0.4 %empty.1.refs_4_ = f32[8,128]{1,0:T(8,128)S(1)} custom-call(bf16[1,256]{1,0:T(2,128)(2,1)S(1)} %broadcast_in_dim.3.trans_weight, bf16[2,256,256]{2,1,0:T(8,128)(2,1)S(1)} %multiply_bitcast_fusion.w_mid, bf16[4,256]{1,0:T(4,128)(2,1)S(1)} %get-tuple-element.12.w_out), custom_call_target="tpu_custom_call" | custom-call | flops 100000 | bytes 1000000 | tf_op jit(solution)/shard_map/empty/pallas_call | solution.py:344
  20.6 1.0 %collective-permute-done.2.refs_2_ = bf16[72,128]{1,0:T(8,128)(2,1)S(1)} collective-permute-done((bf16[72,128]{1,0:T(8,128)(2,1)S(1)}, bf16[72,128]{1,0:T(8,128)(2,1)S(1)}, u32[]{:S(2)}, u32[]{:S(2)}) %collective-permute-start.2) | collective-permute-done | bytes 18464 | tf_op jit(solution)/shard_map/ppermute | solution.py:367
  21.6 0.5 %collective-permute-done.1.refs_1_ = bf16[72,128]{1,0:T(8,128)(2,1)S(1)} collective-permute-done((bf16[72,128]{1,0:T(8,128)(2,1)S(1)}, bf16[72,128]{1,0:T(8,128)(2,1)S(1)}, u32[]{:S(2)}, u32[]{:S(2)}) %collective-permute-start.1) | collective-permute-done | bytes 18464 | tf_op jit(solution)/shard_map/ppermute | solution.py:367
  22.1 0.0 collective-permute-done.refs_0_
  22.1 0.9 %join.1 = bf16[1,4,32,4,128]{4,3,2,1,0:T(4,128)(2,1)} custom-call(bf16[72,128]{1,0:T(8,128)(2,1)S(1)} %collective-permute-done.refs_0_, bf16[72,128]{1,0:T(8,128)(2,1)S(1)} %collective-permute-done.1.refs_1_, bf16[72,128]{1,0:T(8,128)(2,1)S(1)} %collective-permute-done.2.refs_2_, bf16[72,128]{1,0:T(8,128)(2,1)S(1)} %shade.1.refs_3_, f32[8,128]{1,0:T(8,128)S(1)} %empty.1.refs_4_), custom_call_target="tpu_custom_call" | custom-call | tf_op jit(solution)/shard_map/join/pallas_call | solution.py:370
  (3 shorter events, 0.1 us)
Async XLA Ops:
  0.0 10.3 %copy-start.6 = (bf16[2,256,256]{2,1,0:T(8,128)(2,1)S(1)}, bf16[2,256,256]{2,1,0:T(8,128)(2,1)}, u32[]{:S(2)}) copy-start(bf16[2,256,256]{2,1,0:T(8,128)(2,1)} %param.18) | copy-start | bytes 786436
  1.8 7.5 %copy-start = (s32[1,8,8]{2,1,0:T(8,128)S(1)}, s32[1,8,8]{2,1,0:T(8,128)}, u32[]{:S(2)}) copy-start(s32[1,8,8]{2,1,0:T(8,128)} %far_counts.1) | copy-start | bytes 772
  1.8 7.5 %copy-start.2 = (s32[1,8,16]{2,1,0:T(8,128)S(1)}, s32[1,8,16]{2,1,0:T(8,128)}, u32[]{:S(2)}) copy-start(s32[1,8,16]{2,1,0:T(8,128)} %refs_1_.1) | copy-start | bytes 1540
  1.8 7.5 %copy-start.3 = (s32[1,1024]{1,0:T(1,128)S(1)}, s32[1,1024]{1,0:T(1,128)}, u32[]{:S(2)}) copy-start(s32[1,1024]{1,0:T(1,128)} %refs_2_.1) | copy-start | bytes 12292
  1.8 7.5 %copy-start.5 = (s32[8]{0:T(128)S(1)}, s32[8]{0:T(128)}, u32[]{:S(2)}) copy-start(s32[8]{0:T(128)} %refs_3_.1) | copy-start | bytes 100
  1.8 8.4 %copy-start.7 = (bf16[256]{0:T(256)(128)(2,1)S(1)}, bf16[256]{0:T(256)(128)(2,1)}, u32[]{:S(2)}) copy-start(bf16[256]{0:T(256)(128)(2,1)} %param.17) | copy-start | bytes 1540
  1.8 8.4 %copy-start.4 = (bf16[4,256]{1,0:T(4,128)(2,1)S(1)}, bf16[4,256]{1,0:T(4,128)(2,1)}, u32[]{:S(2)}) copy-start(bf16[4,256]{1,0:T(4,128)(2,1)} %far_out.1) | copy-start | bytes 6148
  1.8 14.9 %all-to-all-start = ((bf16[8,72,128]{2,1,0:T(8,128)(2,1)}), bf16[8,72,128]{2,1,0:T(8,128)(2,1)S(1)}, u32[]{:S(2)}, u32[]{:S(2)}) async-start(bf16[8,72,128]{2,1,0:T(8,128)(2,1)} %pack.1), calls=%async_computation | async-start | bytes 294912 | tf_op jit(solution)/shard_map/all_to_all | solution.py:314
  9.3 1.0 %copy-start.1 = (bf16[256,32]{0,1:T(8,128)(2,1)S(1)}, bf16[256,32]{0,1:T(8,128)(2,1)}, u32[]{:S(2)}) copy-start(bf16[256,32]{0,1:T(8,128)(2,1)} %param.16) | copy-start | bytes 49156
  18.3 3.3 %collective-permute-start.2 = (bf16[72,128]{1,0:T(8,128)(2,1)S(1)}, bf16[72,128]{1,0:T(8,128)(2,1)S(1)}, u32[]{:S(2)}, u32[]{:S(2)}) collective-permute-start(bf16[72,128]{1,0:T(8,128)(2,1)S(1)} %shade.1.refs_3_), channel_id=1, source_target_pairs={{0,3},{1,2},{2,1},{3,0},{4,7},{5,6},{6,5},{7,4},{8,11},{9,10},{10,... | collective-permute-start | bytes 55304 | tf_op jit(solution)/shard_map/ppermute | solution.py:367
  18.3 3.8 %collective-permute-start.1 = (bf16[72,128]{1,0:T(8,128)(2,1)S(1)}, bf16[72,128]{1,0:T(8,128)(2,1)S(1)}, u32[]{:S(2)}, u32[]{:S(2)}) collective-permute-start(bf16[72,128]{1,0:T(8,128)(2,1)S(1)} %shade.1.refs_3_), channel_id=1, source_target_pairs={{0,2},{1,3},{2,0},{3,1},{4,6},{5,7},{6,4},{7,5},{8,10},{9,11},{10,... | collective-permute-start | bytes 55304 | tf_op jit(solution)/shard_map/ppermute | solution.py:367
  19.8 2.3 %collective-permute-start = (bf16[72,128]{1,0:T(8,128)(2,1)S(1)}, bf16[72,128]{1,0:T(8,128)(2,1)S(1)}, u32[]{:S(2)}, u32[]{:S(2)}) collective-permute-start(bf16[72,128]{1,0:T(8,128)(2,1)S(1)} %shade.1.refs_3_), channel_id=1, source_target_pairs={{0,1},{1,0},{2,3},{3,2},{4,5},{5,4},{6,7},{7,6},{8,9},{9,8},{10,11... | collective-permute-start | bytes 55304 | tf_op jit(solution)/shard_map/ppermute | solution.py:367
where the time goes:
time: 23.2 us; the launch traced here: 23 us
  starting transfers between devices  9.3 us (40%)
  waiting for transfers between devices  7.72 us (33%)
  Pallas kernels  5.57 us (24%)
    all_to_all x1, starting transfers between devices, compact_device(): got = lax.all_to_all(sends, 'slab', split_axis=0, concat_axis=0, tiled=True)  7.42 us
    all_to_all x1, waiting for transfers between devices, compact_device(): got = lax.all_to_all(sends, 'slab', split_axis=0, concat_axis=0, tiled=True)  6.2 us
    ppermute x3, starting transfers between devices, compact_device(): lax.ppermute(shaded, 'strip', [(s, s ^ k) for s in range(n_strip)])  1.88 us
    pallas_call x1, Pallas kernels, compact_device(): pl.pallas_call(pack_kernel, out_shape=jax.ShapeDtypeStruct((n_slab, messa...  1.74 us
    pallas_call x1, Pallas kernels, compact_device(): pl.pallas_call(shade_kernel, out_shape=jax.ShapeDtypeStruct((items * outs...  1.55 us
    ppermute x3, waiting for transfers between devices, compact_device(): lax.ppermute(shaded, 'strip', [(s, s ^ k) for s in range(n_strip)])  1.53 us
    pallas_call x1, Pallas kernels, compact_device(): pl.pallas_call(functools.partial(plan_kernel, n_slab, slots), out_shape=[...  0.93 us
    pallas_call x1, Pallas kernels, compact_device(): pl.pallas_call(join_kernel, out_shape=jax.ShapeDtypeStruct((1, n_strip, L...  0.87 us
  transfers between devices with their start and end apart: 4, of which 3 were waited for; matrix products, arithmetic and copies ran while one was open for 1% of the time, Pallas kernels for 6%

commit v1 on v0

--- a/solution.py
+++ b/solution.py
@@ -164,7 +164,9 @@
     codes[...] = codev.astype(jnp.float32).astype(jnp.bfloat16)
 
 
-def place_kernel(w_in, trans_weight, far_out, w_first, w_out):
+def place_kernel(w_in, trans_weight, far_out, far_mid, w_first, w_out, w_later, w_mid, sems):
+    copy = pltpu.make_async_copy(far_mid, w_mid, sems.at[0])
+    copy.start()
     feats, hidden = w_in.shape
     half_in = (w_in[...].astype(jnp.float32) * 0.5).astype(jnp.bfloat16)
     half_trans = trans_weight[...].astype(jnp.float32) * 0.5
@@ -175,6 +177,9 @@
         tail = jnp.where(sub // 2 == a, half_trans, 0.0)
         w_first[a, pl.ds(GROUP * feats, 16), :] = tail.astype(jnp.bfloat16)
     w_out[...] = far_out[...]
+    copy.wait()
+    for m in range(w_mid.shape[0]):
+        w_later[m] = (w_mid[m].astype(jnp.float32).T * 0.5).astype(jnp.bfloat16)
 
 
 def silu_half(u):
@@ -295,6 +300,7 @@
     smem = pl.BlockSpec(memory_space=SMEM)
     vmem = pl.BlockSpec(memory_space=VMEM)
     hbm = pl.BlockSpec(memory_space=pltpu.HBM)
+    held = functools.partial(pltpu.with_memory_space_constraint, memory_space=pltpu.HBM)
     small = pltpu.CompilerParams(vmem_limit_bytes=4 * 1024 * 1024)
     message = MOST * feats + ROWS
     sends = pl.pallas_call(
@@ -310,7 +316,7 @@
         ],
         compiler_params=small,
         name="pack",
-    )(*[pltpu.with_memory_space_constraint(a, pltpu.HBM) for a in (pair_counts, colors, transmit)])
+    )(held(pair_counts), held(colors), held(transmit))
     got = lax.all_to_all(sends, "slab", split_axis=0, concat_axis=0, tiled=True)
     hidden = w_in.shape[0]
     rough = pl.CostEstimate(flops=10**5, bytes_accessed=10**6, transcendentals=0)
@@ -328,19 +334,23 @@
         cost_estimate=rough,
         name="plan",
     )(pair_counts, slot_block, assign, depth_rank)
-    w_first, w_last = pl.pallas_call(
+    w_first, w_last, w_later = pl.pallas_call(
         place_kernel,
         out_shape=[
             jax.ShapeDtypeStruct((GROUP, 2 * GROUP * feats, hidden), jnp.bfloat16),
             jax.ShapeDtypeStruct(w_out.shape, jnp.bfloat16),
+            jax.ShapeDtypeStruct(w_mid.shape, jnp.bfloat16),
         ],
-        in_specs=[vmem] * 3,
-        out_specs=[vmem] * 2,
+        in_specs=[vmem] * 3 + [hbm],
+        out_specs=[vmem] * 3,
+        scratch_shapes=[
+            pltpu.VMEM(w_mid.shape, jnp.bfloat16),
+            pltpu.SemaphoreType.DMA((1,)),
+        ],
         compiler_params=small,
         cost_estimate=rough,
         name="place",
-    )(w_in.T, trans_row, w_out)
-    w_later = jnp.swapaxes(w_mid, 1, 2) * jnp.bfloat16(0.5)
+    )(w_in.T, trans_row, w_out, held(w_mid))
     empty = pl.pallas_call(
         empty_kernel,
         out_shape=jax.ShapeDtypeStruct((ROWS, span), jnp.float32),

time: 23.2 us -> 23.2 us (level)
  Pallas kernels: 5.57 us -> 6.58 us
  waiting for transfers between devices: 7.72 us -> 6.84 us
    pallas_call x1, Pallas kernels: 0.04 us -> 1.1 us  [compact_device(): pl.pallas_call(place_kernel, out_shape=[jax.ShapeDtypeStruct((GROUP, 2 *...]
    all_to_all x1, waiting for transfers between devices: 6.2 us -> 5.31 us  [compact_device(): got = lax.all_to_all(sends, 'slab', split_axis=0, concat_axis=0, tiled=True)]
  transfers between devices with their start and end apart: 4 -> 4, of which waited for: 3 -> 3; matrix products, arithmetic and copies ran while one was open for 1% -> 0% of each run, Pallas kernels for 6% -> 11%
where the time goes in v1:
time: 23.2 us; the launch traced here: 22.9 us
  starting transfers between devices  9.3 us (40%)
  waiting for transfers between devices  6.84 us (29%)
  Pallas kernels  6.58 us (28%)
    all_to_all x1, starting transfers between devices, compact_device(): got = lax.all_to_all(sends, 'slab', split_axis=0, concat_axis=0, tiled=True)  7.42 us
    all_to_all x1, waiting for transfers between devices, compact_device(): got = lax.all_to_all(sends, 'slab', split_axis=0, concat_axis=0, tiled=True)  5.31 us
    ppermute x3, starting transfers between devices, compact_device(): lax.ppermute(shaded, 'strip', [(s, s ^ k) for s in range(n_strip)])  1.88 us
    pallas_call x1, Pallas kernels, compact_device(): pl.pallas_call(pack_kernel, out_shape=jax.ShapeDtypeStruct((n_slab, messa...  1.69 us
    pallas_call x1, Pallas kernels, compact_device(): pl.pallas_call(shade_kernel, out_shape=jax.ShapeDtypeStruct((items * outs...  1.55 us
    ppermute x3, waiting for transfers between devices, compact_device(): lax.ppermute(shaded, 'strip', [(s, s ^ k) for s in range(n_strip)])  1.53 us
    pallas_call x1, Pallas kernels, compact_device(): pl.pallas_call(place_kernel, out_shape=[jax.ShapeDtypeStruct((GROUP, 2 *...  1.1 us
    pallas_call x1, Pallas kernels, compact_device(): pl.pallas_call(functools.partial(plan_kernel, n_slab, slots), out_shape=[...  0.93 us
  transfers between devices with their start and end apart: 4, of which 3 were waited for; matrix products, arithmetic and copies ran while one was open for 0% of the time, Pallas kernels for 11%

profile of v1, /device:TPU:0, one launch (start us, length us, event | category | flops | bytes accessed | tf_op | source)
XLA Modules:
  0.0 22.9 jit_solution(8584468511906459325)
XLA Ops:
  0.0 1.7 %pack.1 = bf16[8,72,128]{2,1,0:T(8,128)(2,1)} custom-call(s32[1,8,8]{2,1,0:T(8,128)} %far_counts.1, bf16[1,1,16,32,128]{4,3,2,1,0:T(8,128)(2,1)} %far_colors.1, bf16[1,1,16,128]{3,2,1,0:T(8,128)(2,1)} %far_transmit.1), custom_call_target="tpu_custom_call" | custom-call | tf_op jit(solution)/shard_map/pack/pallas_call | solution.py:306
  1.7 0.0 copy-start
  1.7 0.0 copy-start.2
  1.7 0.0 copy-start.3
  1.7 0.0 copy-start.5
  1.7 0.0 copy-start.6
  1.8 0.0 copy-start.4
  1.8 7.4 %all-to-all-start = ((bf16[8,72,128]{2,1,0:T(8,128)(2,1)}), bf16[8,72,128]{2,1,0:T(8,128)(2,1)S(1)}, u32[]{:S(2)}, u32[]{:S(2)}) async-start(bf16[8,72,128]{2,1,0:T(8,128)(2,1)} %pack.1), calls=%async_computation | async-start | bytes 294912 | tf_op jit(solution)/shard_map/all_to_all | solution.py:320
  9.2 0.0 copy-done
  9.2 0.0 copy-done.2
  9.2 0.0 copy-done.3
  9.2 0.0 copy-done.5
  9.2 0.0 copy-start.1
  9.2 0.9 %plan.1 = (s32[3,16,128]{2,1,0:T(8,128)S(1)}, bf16[8,128]{1,0:T(8,128)(2,1)S(1)}) custom-call(s32[1,8,8]{2,1,0:T(8,128)S(1)} %copy-done, s32[1,8,16]{2,1,0:T(8,128)S(1)} %copy-done.2, s32[1,1024]{1,0:T(1,128)S(1)} %copy-done.3, s32[8]{0:T(128)S(1)} %copy-done.5), custom_call_target="tpu_custom_call" | custom-call | flops 100000 | bytes 1000000 | tf_op jit(solution)/shard_map/plan/pallas_call | solution.py:325
  10.2 0.0 copy-done.6
  10.2 0.0 copy-done.4
  10.2 0.0 copy-done.1
  10.2 1.1 %place.1 = (bf16[4,256,256]{2,1,0:T(8,128)(2,1)S(1)}, bf16[4,256]{1,0:T(4,128)(2,1)S(1)}, bf16[2,256,256]{2,1,0:T(8,128)(2,1)S(1)}) custom-call(bf16[32,256]{1,0:T(8,128)(2,1)S(1)} %bitcast.1, bf16[1,256]{1,0:T(2,128)(2,1)S(1)} %broadcast_in_dim.3.trans_weight, bf16[4,256]{1,0:T(4,128)(2,1)S(1)} %copy-done.4, bf16[2,256,256]{2,1,0:T(8,128)(2,1)} %far_mid.1), custom_call_target="tpu_custom_call" | custom-call | flops 100000 | bytes 1000000 | tf_op jit(solution)/shard_map/place/pallas_call | solution.py:337
  11.3 5.3 %all-to-all-done.got = bf16[8,72,128]{2,1,0:T(8,128)(2,1)S(1)} async-done(((bf16[8,72,128]{2,1,0:T(8,128)(2,1)}), bf16[8,72,128]{2,1,0:T(8,128)(2,1)S(1)}, u32[]{:S(2)}, u32[]{:S(2)}) %all-to-all-start) | async-done | bytes 147488 | tf_op jit(solution)/shard_map/all_to_all | solution.py:320
  16.7 1.6 %shade.1.refs_3_ = bf16[72,128]{1,0:T(8,128)(2,1)S(1)} custom-call(s32[3,16,128]{2,1,0:T(8,128)S(1)} %get-tuple-element.10.rows, bf16[8,128]{1,0:T(8,128)(2,1)S(1)} %get-tuple-element.11.codes, bf16[8,72,128]{2,1,0:T(8,128)(2,1)S(1)} %all-to-all-done.got, bf16[4,256,256]{2,1,0:T(8,128)(2,1)S(1)} %get-tuple-element.12.w_first, ...), custom_call_target="tpu_custom_call" | custom-call | tf_op jit(solution)/shard_map/shade/pallas_call | solution.py:363
  18.2 0.0 collective-permute-start.2
  18.2 1.6 %collective-permute-start.1 = (bf16[72,128]{1,0:T(8,128)(2,1)S(1)}, bf16[72,128]{1,0:T(8,128)(2,1)S(1)}, u32[]{:S(2)}, u32[]{:S(2)}) collective-permute-start(bf16[72,128]{1,0:T(8,128)(2,1)S(1)} %shade.1.refs_3_), channel_id=1, source_target_pairs={{0,2},{1,3},{2,0},{3,1},{4,6},{5,7},{6,4},{7,5},{8,10},{9,11},{10,... | collective-permute-start | bytes 55304 | tf_op jit(solution)/shard_map/ppermute | solution.py:377
  19.8 0.3 %collective-permute-start = (bf16[72,128]{1,0:T(8,128)(2,1)S(1)}, bf16[72,128]{1,0:T(8,128)(2,1)S(1)}, u32[]{:S(2)}, u32[]{:S(2)}) collective-permute-start(bf16[72,128]{1,0:T(8,128)(2,1)S(1)} %shade.1.refs_3_), channel_id=1, source_target_pairs={{0,1},{1,0},{2,3},{3,2},{4,5},{5,4},{6,7},{7,6},{8,9},{9,8},{10,11... | collective-permute-start | bytes 55304 | tf_op jit(solution)/shard_map/ppermute | solution.py:377
  20.1 0.4 %empty.1.refs_4_ = f32[8,128]{1,0:T(8,128)S(1)} custom-call(bf16[1,256]{1,0:T(2,128)(2,1)S(1)} %broadcast_in_dim.3.trans_weight, bf16[2,256,256]{2,1,0:T(8,128)(2,1)S(1)} %get-tuple-element.13.w_mid, bf16[4,256]{1,0:T(4,128)(2,1)S(1)} %get-tuple-element.14.w_out), custom_call_target="tpu_custom_call" | custom-call | flops 100000 | bytes 1000000 | tf_op jit(solution)/shard_map/empty/pallas_call | solution.py:354
  20.5 1.0 %collective-permute-done.2.refs_2_ = bf16[72,128]{1,0:T(8,128)(2,1)S(1)} collective-permute-done((bf16[72,128]{1,0:T(8,128)(2,1)S(1)}, bf16[72,128]{1,0:T(8,128)(2,1)S(1)}, u32[]{:S(2)}, u32[]{:S(2)}) %collective-permute-start.2) | collective-permute-done | bytes 18464 | tf_op jit(solution)/shard_map/ppermute | solution.py:377
  21.6 0.5 %collective-permute-done.1.refs_1_ = bf16[72,128]{1,0:T(8,128)(2,1)S(1)} collective-permute-done((bf16[72,128]{1,0:T(8,128)(2,1)S(1)}, bf16[72,128]{1,0:T(8,128)(2,1)S(1)}, u32[]{:S(2)}, u32[]{:S(2)}) %collective-permute-start.1) | collective-permute-done | bytes 18464 | tf_op jit(solution)/shard_map/ppermute | solution.py:377
  22.0 0.0 collective-permute-done.refs_0_
  22.0 0.9 %join.1 = bf16[1,4,32,4,128]{4,3,2,1,0:T(4,128)(2,1)} custom-call(bf16[72,128]{1,0:T(8,128)(2,1)S(1)} %collective-permute-done.refs_0_, bf16[72,128]{1,0:T(8,128)(2,1)S(1)} %collective-permute-done.1.refs_1_, bf16[72,128]{1,0:T(8,128)(2,1)S(1)} %collective-permute-done.2.refs_2_, bf16[72,128]{1,0:T(8,128)(2,1)S(1)} %shade.1.refs_3_, f32[8,128]{1,0:T(8,128)S(1)} %empty.1.refs_4_), custom_call_target="tpu_custom_call" | custom-call | tf_op jit(solution)/shard_map/join/pallas_call | solution.py:380
  (1 shorter events, 0.0 us)
Async XLA Ops:
  1.7 7.5 %copy-start = (s32[1,8,8]{2,1,0:T(8,128)S(1)}, s32[1,8,8]{2,1,0:T(8,128)}, u32[]{:S(2)}) copy-start(s32[1,8,8]{2,1,0:T(8,128)} %far_counts.1) | copy-start | bytes 772
  1.7 7.5 %copy-start.2 = (s32[1,8,16]{2,1,0:T(8,128)S(1)}, s32[1,8,16]{2,1,0:T(8,128)}, u32[]{:S(2)}) copy-start(s32[1,8,16]{2,1,0:T(8,128)} %refs_1_.1) | copy-start | bytes 1540
  1.7 7.5 %copy-start.3 = (s32[1,1024]{1,0:T(1,128)S(1)}, s32[1,1024]{1,0:T(1,128)}, u32[]{:S(2)}) copy-start(s32[1,1024]{1,0:T(1,128)} %refs_2_.1) | copy-start | bytes 12292
  1.7 7.5 %copy-start.5 = (s32[8]{0:T(128)S(1)}, s32[8]{0:T(128)}, u32[]{:S(2)}) copy-start(s32[8]{0:T(128)} %refs_3_.1) | copy-start | bytes 100
  1.7 8.4 %copy-start.6 = (bf16[256]{0:T(256)(128)(2,1)S(1)}, bf16[256]{0:T(256)(128)(2,1)}, u32[]{:S(2)}) copy-start(bf16[256]{0:T(256)(128)(2,1)} %param.17) | copy-start | bytes 1540
  1.8 8.4 %copy-start.4 = (bf16[4,256]{1,0:T(4,128)(2,1)S(1)}, bf16[4,256]{1,0:T(4,128)(2,1)}, u32[]{:S(2)}) copy-start(bf16[4,256]{1,0:T(4,128)(2,1)} %far_out.1) | copy-start | bytes 6148
  1.8 14.9 %all-to-all-start = ((bf16[8,72,128]{2,1,0:T(8,128)(2,1)}), bf16[8,72,128]{2,1,0:T(8,128)(2,1)S(1)}, u32[]{:S(2)}, u32[]{:S(2)}) async-start(bf16[8,72,128]{2,1,0:T(8,128)(2,1)} %pack.1), calls=%async_computation | async-start | bytes 294912 | tf_op jit(solution)/shard_map/all_to_all | solution.py:320
  9.2 1.0 %copy-start.1 = (bf16[256,32]{0,1:T(8,128)(2,1)S(1)}, bf16[256,32]{0,1:T(8,128)(2,1)}, u32[]{:S(2)}) copy-start(bf16[256,32]{0,1:T(8,128)(2,1)} %param.16) | copy-start | bytes 49156
  18.2 3.4 %collective-permute-start.2 = (bf16[72,128]{1,0:T(8,128)(2,1)S(1)}, bf16[72,128]{1,0:T(8,128)(2,1)S(1)}, u32[]{:S(2)}, u32[]{:S(2)}) collective-permute-start(bf16[72,128]{1,0:T(8,128)(2,1)S(1)} %shade.1.refs_3_), channel_id=1, source_target_pairs={{0,3},{1,2},{2,1},{3,0},{4,7},{5,6},{6,5},{7,4},{8,11},{9,10},{10,... | collective-permute-start | bytes 55304 | tf_op jit(solution)/shard_map/ppermute | solution.py:377
  18.2 3.8 %collective-permute-start.1 = (bf16[72,128]{1,0:T(8,128)(2,1)S(1)}, bf16[72,128]{1,0:T(8,128)(2,1)S(1)}, u32[]{:S(2)}, u32[]{:S(2)}) collective-permute-start(bf16[72,128]{1,0:T(8,128)(2,1)S(1)} %shade.1.refs_3_), channel_id=1, source_target_pairs={{0,2},{1,3},{2,0},{3,1},{4,6},{5,7},{6,4},{7,5},{8,10},{9,11},{10,... | collective-permute-start | bytes 55304 | tf_op jit(solution)/shard_map/ppermute | solution.py:377
  19.8 2.3 %collective-permute-start = (bf16[72,128]{1,0:T(8,128)(2,1)S(1)}, bf16[72,128]{1,0:T(8,128)(2,1)S(1)}, u32[]{:S(2)}, u32[]{:S(2)}) collective-permute-start(bf16[72,128]{1,0:T(8,128)(2,1)S(1)} %shade.1.refs_3_), channel_id=1, source_target_pairs={{0,1},{1,0},{2,3},{3,2},{4,5},{5,4},{6,7},{7,6},{8,9},{9,8},{10,11... | collective-permute-start | bytes 55304 | tf_op jit(solution)/shard_map/ppermute | solution.py:377
